TPU v7x, 32 devices: a whole 2x2x4 slice. The times are simulated.
32 devices in a mesh: groups: 2 (over y), segment: 8 (over z, x), template: 2 (over core).
Axes of the slice: x: 2, y: 2, z: 4, core: 2. Of those that a mesh axis runs over, the one named last changes fastest.
Arguments:
- strain_frames: bfloat16 [64, 16384], P('segment'), may hold values from -6 to 6
- frame_slot: int32 [8, 8], replicated, may hold values from 0 to 7, as said below
- templates: bfloat16 [4, 2, 131072], P(('groups', 'template'), None, 'segment'), parts along dimension 0, may hold values from -6 to 6
- bin_edges: int32 [4, 3], P(('groups', 'template')), parts along dimension 0, may hold values from 16384 to 114687, as said below
Outputs:
- snr_series: bfloat16 [8, 4, 131072], P('segment', ('groups', 'template')), parts along dimension 1
- chisq_series: bfloat16 [8, 4, 131072], P('segment', ('groups', 'template')), parts along dimension 1
- peak_newsnr: float32 [8, 4], P('segment', ('groups', 'template')), parts along dimension 1
There are 2 independent parts, one for each index of `groups`. A program takes and returns all parts, laid end to end along the dimension named above; an argument that names none is the same for every part. Nothing has to cross between parts.
Inputs may be any that keep to these rules, and one draw needn't show every extreme that they name: Each column frame_slot[:, j] is a permutation of 0 to 7. `bin_edges`: edge number e of a template lies in [(2 e + 1) * 16384, (2 e + 3) * 16384), so the edges rise.
All inputs are finite; a program needn't handle non-finite values.
Results may differ from a plain program's by a relative error of at most 0.011.
Values may be sent and summed in bfloat16 or wider, within the bound.
A program may use at most 64 MiB of HBM per device.

v0:
```python
import math
import jax
import jax.numpy as jnp
from jax import lax
from jax.sharding import PartitionSpec as P

RADIX_A = 64
RADIX_B = 32
RADIX_C = 128


def dft_table(length, orient):
    counter = jnp.arange(length, dtype=jnp.int32)
    product = counter[:, None] * counter[None, :] % length
    angles = orient * 2.0 * math.pi / length * product.astype(jnp.float32)
    cosine = jnp.cos(angles)
    sine = jnp.sin(angles)
    upper = jnp.stack([cosine, -sine], axis=1)
    lower = jnp.stack([sine, cosine], axis=1)
    return jnp.stack([upper, lower], axis=0).astype(jnp.bfloat16)


def rotate(values, phase_index, modulus, orient):
    angles = orient * 2.0 * math.pi / modulus * (phase_index % modulus).astype(jnp.float32)
    cosine = jnp.cos(angles)
    sine = jnp.sin(angles)
    real_part = values[0] * cosine - values[1] * sine
    imag_part = values[0] * sine + values[1] * cosine
    return jnp.stack([real_part, imag_part]).astype(jnp.bfloat16)


def later_passes(level_one, orient, table_three):
    length = RADIX_A * RADIX_B * RADIX_C
    inner = RADIX_B * RADIX_C
    grid_one = (
        jnp.arange(RADIX_A, dtype=jnp.int32)[:, None] * jnp.arange(inner, dtype=jnp.int32)[None, :]
    )
    turned = rotate(level_one, grid_one, length, orient).reshape(2, RADIX_A, RADIX_B, RADIX_C)
    level_two = jnp.einsum(
        "cjdp,dkpr->ckjr", dft_table(RADIX_B, orient), turned, preferred_element_type=jnp.float32
    )
    grid_two = (
        jnp.arange(RADIX_B, dtype=jnp.int32)[:, None]
        * jnp.arange(RADIX_C, dtype=jnp.int32)[None, :]
    )
    turned_two = rotate(level_two, grid_two, inner, orient)
    level_three = jnp.einsum(
        "cldr,dkjr->ckjl", table_three, turned_two, preferred_element_type=jnp.float32
    )
    rows = table_three.shape[1]
    return jnp.transpose(level_three, (0, 3, 2, 1)).reshape(2, rows * inner * RADIX_A // RADIX_C)


def forward_spectrum(real_signal):
    inner = RADIX_B * RADIX_C
    start = real_signal.reshape(RADIX_A, inner)
    table_one = dft_table(RADIX_A, -1.0)[:, :, 0, :]
    level_one = jnp.einsum("ckp,pq->ckq", table_one, start, preferred_element_type=jnp.float32)
    table_three = dft_table(RADIX_C, -1.0)[:, : RADIX_C // 2]
    return later_passes(level_one, -1.0, table_three)


def inverse_kept(masked):
    inner = RADIX_B * RADIX_C
    start = masked.reshape(2, RADIX_A // 2, inner)
    table_one = dft_table(RADIX_A, 1.0)[:, :, :, : RADIX_A // 2]
    level_one = jnp.einsum("ckdp,dpq->ckq", table_one, start, preferred_element_type=jnp.float32)
    table_three = dft_table(RADIX_C, 1.0)[:, RADIX_C // 4 : RADIX_C // 4 + RADIX_C // 2]
    return later_passes(level_one, 1.0, table_three)


def filter_template(spectrum, template, edges):
    length = RADIX_A * RADIX_B * RADIX_C
    kept = length // 2
    temp_real = template[0].astype(jnp.float32)
    temp_imag = template[1].astype(jnp.float32)
    corr_real = spectrum[0] * temp_real + spectrum[1] * temp_imag
    corr_imag = spectrum[1] * temp_real - spectrum[0] * temp_imag
    power = temp_real * temp_real + temp_imag * temp_imag
    total = jnp.sum(power)
    bin_index = jnp.arange(kept, dtype=jnp.int32)
    label = (
        (bin_index >= edges[0]).astype(jnp.int32)
        + (bin_index >= edges[1]).astype(jnp.int32)
        + (bin_index >= edges[2]).astype(jnp.int32)
    )
    pieces = []
    shares = []
    for number in range(4):
        inside = (label == number).astype(jnp.float32)
        shares.append(jnp.sum(power * inside) / total)
        masked = jnp.stack([corr_real * inside, corr_imag * inside]).astype(jnp.bfloat16)
        pieces.append(inverse_kept(masked) / length)
    summed = pieces[0] + pieces[1] + pieces[2] + pieces[3]
    scale = length / total
    snr = jnp.sqrt((summed[0] * summed[0] + summed[1] * summed[1]) * scale)
    chisq = jnp.zeros_like(snr)
    for number in range(4):
        diff_real = pieces[number][0] - shares[number] * summed[0]
        diff_imag = pieces[number][1] - shares[number] * summed[1]
        chisq = chisq + diff_real * diff_real + diff_imag * diff_imag
    chisq = chisq * scale
    reduced = chisq / 6.0
    weighted = snr * ((1.0 + reduced * reduced * reduced) / 2.0) ** (-1.0 / 6.0)
    newsnr = jnp.where(reduced > 1.0, weighted, snr)
    return (snr.astype(jnp.bfloat16), chisq.astype(jnp.bfloat16), jnp.max(newsnr))


def local(strain_frames, frame_slot, templates, bin_edges):
    segments_count = lax.axis_size("segment")
    position = lax.axis_index("segment")
    frame_length = strain_frames.shape[1]
    length = RADIX_A * RADIX_B * RADIX_C
    kept = length // 2
    counter = jnp.arange(segments_count, dtype=jnp.int32)
    slot_now = lax.dynamic_slice_in_dim(frame_slot, position, 1, 1)[:, 0]
    next_index = jnp.minimum(position + 1, segments_count - 1)
    slot_next = lax.dynamic_slice_in_dim(frame_slot, next_index, 1, 1)[:, 0]

    def arrange(slots, frames):
        selector = (counter[:, None] == slots[None, :]).astype(jnp.bfloat16)
        return (
            jnp.dot(selector, frames, preferred_element_type=jnp.float32)
            .astype(jnp.bfloat16)
            .reshape(kept)
        )

    following_rows = jnp.concatenate(
        [strain_frames[1:], jnp.zeros((1, frame_length), jnp.bfloat16)], axis=0
    )
    outgoing = jnp.stack([strain_frames, following_rows], axis=1)
    received = lax.all_to_all(outgoing, "segment", split_axis=0, concat_axis=0, tiled=True)
    leading = arrange(slot_now, received[:, 0])
    trailing = arrange(slot_next, received[:, 1])
    segment_data = jnp.concatenate([leading, trailing])
    whole_templates = lax.all_gather(templates, "segment", axis=2, tiled=True)
    spectrum = forward_spectrum(segment_data)
    snr_one, chisq_one, peak_one = filter_template(spectrum, whole_templates[0], bin_edges[0])
    snr_rows = [snr_one]
    chisq_rows = [chisq_one]
    peak_rows = [peak_one]
    snr_series = jnp.stack(snr_rows)[None]
    chisq_series = jnp.stack(chisq_rows)[None]
    peak_newsnr = jnp.stack(peak_rows)[None]
    return (snr_series, chisq_series, peak_newsnr)


def solution(mesh):
    in_specs = (
        P("segment", None),
        P(),
        P(("groups", "template"), None, "segment"),
        P(("groups", "template"), None),
    )
    out_specs = (
        P("segment", ("groups", "template"), None),
        P("segment", ("groups", "template"), None),
        P("segment", ("groups", "template")),
    )
    return jax.shard_map(local, mesh=mesh, in_specs=in_specs, out_specs=out_specs, check_vma=False)
```

profile of v0, /device:TPU:0, one launch (start us, length us, event | category | flops | bytes accessed | tf_op | source)
XLA Modules:
  0.0 121.7 jit_solution(296445114597201190)
XLA Ops:
  0.6 1.0 slice.196
  1.7 1.0 pad_maximum_fusion
  2.7 1.3 %copy.65 = bf16[8,2,16384]{2,1,0:T(2,128)(2,1)} copy(bf16[8,2,16384]{2,0,1:T(8,128)(2,1)S(1)} %pad_maximum_fusion) | data formatting | bytes 1048576 | tf_op jit(solution)/shard_map/stack | solution.py:131
  4.1 7.3 %all-to-all-start = ((bf16[8,2,16384]{2,1,0:T(2,128)(2,1)}), bf16[8,2,16384]{2,1,0:T(2,128)(2,1)S(1)}, u32[]{:S(2)}, u32[]{:S(2)}) async-start(bf16[8,2,16384]{2,1,0:T(2,128)(2,1)} %copy.65), calls=%async_computation | async-start | bytes 1048576 | tf_op jit(solution)/shard_map/all_to_all | solution.py:132
  14.4 35.5 %all_gather.3 = bf16[1,2,131072]{2,1,0:T(2,128)(2,1)S(1)} all-gather(bf16[1,2,16384]{2,1,0:T(2,128)(2,1)S(1)} %copy-done.3), channel_id=1, replica_groups=mesh['groups'=2,'segment'=8,'template'=2] {'segment'}, dimensions={2}, use_global_device_ids=true | all-gather | bytes 589824 | tf_op jit(solution)/shard_map/all_gather | solution.py:136
  49.9 4.1 %fusion.81 = (f32[131072]{0:T(1024)S(1)}, f32[131072]{0:T(1024)S(1)}, f32[]{:T(128)}, f32[1,1,131072]{2,1,0:T(1,128)S(1)}) fusion(bf16[1,2,131072]{2,1,0:T(2,128)(2,1)S(1)} %all_gather.3), kind=kLoop, calls=%fused_computation.186 | loop fusion | flops 786431 | bytes 2097156 | tf_op jit(solution)/shard_map/convert_element_type | solution.py:75
  54.0 2.9 %select_reduce_fusion.3 = (f32[]{:T(128)}, f32[]{:T(128)}, f32[]{:T(128)}, f32[]{:T(128)}) fusion(f32[131072]{0:T(1024)S(1)} %bitcast.310, s32[]{:T(128)} %bitcast.4, s32[]{:T(128)} %bitcast.3, s32[]{:T(128)} %bitcast.2), kind=kLoop, calls=%fused_computation.155 | loop fusion | flops 2621436 | bytes 524316 | tf_op jit(solution)/shard_map/reduce_sum | solution.py:91
  67.9 4.8 %fusion.79 = (bf16[8,8,32,128]{3,1,2,0:T(8,128)(2,1)S(1)}, bf16[8,8,32,128]{3,1,2,0:T(8,128)(2,1)S(1)}) fusion(f32[2,64,4096]{2,1,0:T(8,128)S(1)} %fusion.57), kind=kLoop, calls=%fused_computation.184 | loop fusion | flops 5767168 | bytes 3145728
  74.3 1.1 copy.71
  75.8 1.1 copy.70
  77.3 3.3 %select_convert_fusion.5 = (bf16[1,32,4096]{2,1,0:T(8,128)(2,1)S(1)}, bf16[1,32,4096]{2,1,0:T(8,128)(2,1)S(1)}, bf16[1,32,4096]{2,1,0:T(8,128)(2,1)S(1)}, bf16[1,32,4096]{2,1,0:T(8,128)(2,1)S(1)}) fusion(s32[]{:T(128)} %bitcast.4, s32[]{:T(128)} %bitcast.3, s32[]{:T(128)} %bitcast.2, f32[1,32,4096]{2,1,0:T(8,128)S(1)} %squeeze.55, ...), kind=kLoop, calls=%fused_computation.170 | loop fusion | flops 2752512 | bytes 3145740 | tf_op jit(solution)/shard_map/convert.25
  80.5 2.3 %select_convert_fusion.6 = (bf16[1,32,4096]{2,1,0:T(8,128)(2,1)S(1)}, bf16[1,32,4096]{2,1,0:T(8,128)(2,1)S(1)}, bf16[1,32,4096]{2,1,0:T(8,128)(2,1)S(1)}, bf16[1...) fusion(bf16[1,32,4096]{2,1,0:T(8,128)(2,1)S(1)} %get-tuple-element.42, ...), kind=kLoop, calls=%fused_computation.171 | loop fusion | flops 2490368 | bytes 2097164 | tf_op jit(solution)/shard_map/convert.50
  83.3 4.6 %fusion.49 = (bf16[8,8,32,128]{3,1,2,0:T(8,128)(2,1)S(1)}, bf16[8,8,32,128]{3,1,2,0:T(8,128)(2,1)S(1)}) fusion(f32[2,64,4096]{2,1,0:T(8,128)S(1)} %convolution_bitcast_fusion.3), kind=kLoop, calls=%fused_computation.114 | loop fusion | flops 5767168 | bytes 3145728
  88.6 4.6 %fusion.51 = (bf16[8,8,32,128]{3,1,2,0:T(8,128)(2,1)S(1)}, bf16[8,8,32,128]{3,1,2,0:T(8,128)(2,1)S(1)}) fusion(f32[2,64,4096]{2,1,0:T(8,128)S(1)} %convolution_bitcast_fusion.2), kind=kLoop, calls=%fused_computation.116 | loop fusion | flops 5767168 | bytes 3145728
  94.0 4.6 %fusion.53 = (bf16[8,8,32,128]{3,1,2,0:T(8,128)(2,1)S(1)}, bf16[8,8,32,128]{3,1,2,0:T(8,128)(2,1)S(1)}) fusion(f32[2,64,4096]{2,1,0:T(8,128)S(1)} %convolution_bitcast_fusion.1), kind=kLoop, calls=%fused_computation.118 | loop fusion | flops 5767168 | bytes 3145728
  99.3 4.8 %fusion.55 = (bf16[8,8,32,128]{3,1,2,0:T(8,128)(2,1)S(1)}, bf16[8,8,32,128]{3,1,2,0:T(8,128)(2,1)S(1)}) fusion(f32[2,64,4096]{2,1,0:T(8,128)S(1)} %convolution_bitcast_fusion), kind=kLoop, calls=%fused_computation.120 | loop fusion | flops 5767168 | bytes 3145728
  106.3 1.3 %subtract_convert_fusion.4 = (bf16[1,64,32,128]{3,2,0,1:T(8,128)(2,1)S(1)}, bf16[1,64,32,128]{3,2,0,1:T(8,128)(2,1)S(1)}, bf16[1,64,32,128]{3,2,0,1:T(8,128)(2,1...) fusion(f32[2,64,32,128]{3,2,0,1:T(8,128)S(1)} %convolution_bitc, ...), kind=kLoop, calls=%fused_computation.90 | loop fusion | flops 8388608 | bytes 12615680 | tf_op jit(solution)/shard_map/convert.19
  109.5 2.4 %broadcast_multiply_fusion = (f32[1,64,32,64]{1,2,0,3:T(8,128)S(1)}, bf16[1,64,32,64]{1,2,0,3:T(8,128)(2,1)}, bf16[1,64,32,64]{1,2,0,3:T(8,128)(2,1)}, f32[1,64,32,64]{1,2,0,3:T(8,128)S(1)}) fusion(f32[]{:T(128)S(6)} %div.55, f32[2,64,32,64]{1,2,0,3:T(8,128)S(1)} %get-tuple-element.79, f32[]{:T(128)S(6)} %div.59, f32[2,64,32,64]{1,2,0,3:T(8,128)S(1)} %fusion.1, ...), kind=kLoop, calls=%fused_computation.151 | loop fusion | flops 5111808 | bytes 6815764 | tf_op jit(solution)/shard_map/div | solution.py:103
  112.0 1.1 copy.86
  114.0 2.1 %copy.85 = bf16[1,64,32,64]{3,2,1,0:T(8,128)(2,1)S(1)} copy(bf16[1,64,32,64]{1,2,0,3:T(8,128)(2,1)} %get-tuple-element.12) | data formatting | bytes 524288 | tf_op jit(solution)/shard_map/convert_element_type | solution.py:106
  116.2 1.1 reshape.1302
  117.3 1.1 copy.84
  118.3 1.1 sqrt.17
  119.4 1.1 copy.87
  (90 shorter events, 19.3 us)
Async XLA Ops:
  1.6 12.1 %copy-start.5 = (s32[1,3]{1,0:T(1,128)S(1)}, s32[1,3]{1,0:T(1,128)}, u32[]{:S(2)}) copy-start(s32[1,3]{1,0:T(1,128)} %param.7) | copy-start | bytes 40
  1.7 12.7 %copy-start.3 = (bf16[1,2,16384]{2,1,0:T(2,128)(2,1)S(1)}, bf16[1,2,16384]{2,1,0:T(2,128)(2,1)}, u32[]{:S(2)}) copy-start(bf16[1,2,16384]{2,1,0:T(2,128)(2,1)} %param.6) | copy-start | bytes 196612
  4.1 61.2 %all-to-all-start = ((bf16[8,2,16384]{2,1,0:T(2,128)(2,1)}), bf16[8,2,16384]{2,1,0:T(2,128)(2,1)S(1)}, u32[]{:S(2)}, u32[]{:S(2)}) async-start(bf16[8,2,16384]{2,1,0:T(2,128)(2,1)} %copy.65), calls=%async_computation | async-start | bytes 1048576 | tf_op jit(solution)/shard_map/all_to_all | solution.py:132
  49.9 14.7 %copy-start.4 = (s32[8,8]{1,0:T(8,128)S(1)}, s32[8,8]{1,0:T(8,128)}, u32[]{:S(2)}) copy-start(s32[8,8]{1,0:T(8,128)} %param.5) | copy-start | bytes 772
  75.8 1.5 %copy-start = (f32[1,32,4096]{2,1,0:T(8,128)S(1)}, f32[1,32,4096]{2,1,0:T(8,128)}, u32[]{:S(2)}) copy-start(f32[1,32,4096]{2,1,0:T(8,128)} %reshape.1209) | copy-start | bytes 1572868
  113.0 4.2 %copy-start.1 = (bf16[1,64,32,64]{1,2,0,3:T(8,128)(2,1)S(1)}, bf16[1,64,32,64]{1,2,0,3:T(8,128)(2,1)}, u32[]{:S(2)}) copy-start(bf16[1,64,32,64]{1,2,0,3:T(8,128)(2,1)} %get-tuple-element.31) | copy-start | bytes 786436
  119.4 1.3 %copy-start.2 = (f32[131072]{0:T(1024)S(1)}, f32[131072]{0:T(1024)}, u32[]{:S(2)}) copy-start(f32[131072]{0:T(1024)} %reshape.1304) | copy-start | bytes 1572868
where the time goes:
time: 122 us
  other arithmetic  44.6 us (37%)
  blocking collectives  35.5 us (29%)
  local copies, waits for them, and re-layouts  19.4 us (16%)
  matrix products  7.79 us (6%)
  starting transfers between devices  7.25 us (6%)
  between operations  7.15 us (6%)
    all_gather x1, blocking collectives, local(): whole_templates = lax.all_gather(templates, 'segment', axis=2, tiled=True)  35.5 us
    unnamed x5, other arithmetic  23.3 us
    another operation x19, other arithmetic  9.6 us
    all_to_all x1, starting transfers between devices, local(): lax.all_to_all(outgoing, 'segment', split_axis=0, concat_axis=0, tiled=True)  7.25 us
    convert_element_type x1, other arithmetic, filter_template(): temp_real = template[0].astype(jnp.float32)  4.07 us
    convert_element_type x2, local copies, waits for them, and re-layouts, filter_template(): chisq.astype(jnp.bfloat16)  3.2 us
    reduce_sum x1, other arithmetic, filter_template(): shares.append(jnp.sum(power * inside) / total)  2.89 us
  transfers between devices with their start and end apart: 1, of which 0 were waited for; matrix products, arithmetic and copies ran while one was open for 10% of the time, Pallas kernels for 0%

commit v1 on v0

--- a/solution.py
+++ b/solution.py
@@ -133,7 +133,14 @@
     leading = arrange(slot_now, received[:, 0])
     trailing = arrange(slot_next, received[:, 1])
     segment_data = jnp.concatenate([leading, trailing])
-    whole_templates = lax.all_gather(templates, "segment", axis=2, tiled=True)
+    ways, here = (lax.axis_size("segment"), lax.axis_index("segment"))
+    whole_templates, reach = (templates, 1)
+    while reach < ways:
+        theirs = lax.ppermute(whole_templates, "segment", [(d, d ^ reach) for d in range(ways)])
+        mine_first = jnp.concatenate([whole_templates, theirs], axis=2)
+        theirs_first = jnp.concatenate([theirs, whole_templates], axis=2)
+        whole_templates = jnp.where(here & reach == 0, mine_first, theirs_first)
+        reach = 2 * reach
     spectrum = forward_spectrum(segment_data)
     snr_one, chisq_one, peak_one = filter_template(spectrum, whole_templates[0], bin_edges[0])
     snr_rows = [snr_one]

time: 122 us -> 111 us (0.910)
  blocking collectives: 35.5 us -> 0 us
  waiting for transfers between devices: 0.01 us -> 16.8 us
  starting transfers between devices: 7.25 us -> 13 us
  other arithmetic: 44.6 us -> 46.4 us
    all_gather x1 -> x0, blocking collectives: 35.5 us -> none  [local(): whole_templates = lax.all_gather(templates, 'segment', axis=2, tiled=True)]
    ppermute x0 -> x3, waiting for transfers between devices: none -> 16.8 us  [local(): lax.ppermute(whole_templates, 'segment', [(d, d ^ reach) for d in range(w...]
    ppermute x0 -> x3, starting transfers between devices: none -> 8.08 us  [local(): lax.ppermute(whole_templates, 'segment', [(d, d ^ reach) for d in range(w...]
    all_to_all x1, starting transfers between devices: 7.25 us -> 4.88 us  [local(): lax.all_to_all(outgoing, 'segment', split_axis=0, concat_axis=0, tiled=True)]
    select_n x0 -> x4, other arithmetic: none -> 1.64 us  [local(): whole_templates = jnp.where(here & reach == 0, mine_first, theirs_first)]
  transfers between devices with their start and end apart: 1 -> 4, of which waited for: 0 -> 2; matrix products, arithmetic and copies ran while one was open for 10% -> 16% of each run, Pallas kernels for 0% -> 0%
where the time goes in v1:
time: 111 us
  other arithmetic  46.4 us (42%)
  local copies, waits for them, and re-layouts  19.5 us (18%)
  waiting for transfers between devices  16.8 us (15%)
  starting transfers between devices  13 us (12%)
  matrix products  7.97 us (7%)
  between operations  7.28 us (7%)
    unnamed x5, other arithmetic  23.1 us
    ppermute x3, waiting for transfers between devices, local(): lax.ppermute(whole_templates, 'segment', [(d, d ^ reach) for d in range(w...  16.8 us
    another operation x19, other arithmetic  9.54 us
    ppermute x3, starting transfers between devices, local(): lax.ppermute(whole_templates, 'segment', [(d, d ^ reach) for d in range(w...  8.08 us
    all_to_all x1, starting transfers between devices, local(): lax.all_to_all(outgoing, 'segment', split_axis=0, concat_axis=0, tiled=True)  4.88 us
    convert_element_type x1, other arithmetic, filter_template(): temp_real = template[0].astype(jnp.float32)  4.08 us
    convert_element_type x2, local copies, waits for them, and re-layouts, filter_template(): chisq.astype(jnp.bfloat16)  3.2 us
    reduce_sum x1, other arithmetic, filter_template(): shares.append(jnp.sum(power * inside) / total)  2.91 us
  transfers between devices with their start and end apart: 4, of which 2 were waited for; matrix products, arithmetic and copies ran while one was open for 16% of the time, Pallas kernels for 0%

profile of v1, /device:TPU:0, one launch (start us, length us, event | category | flops | bytes accessed | tf_op | source)
XLA Modules:
  0.0 110.9 jit_solution(11055131157901920321)
XLA Ops:
  0.6 3.0 %collective-permute-start = (bf16[1,2,16384]{2,1,0:T(2,128)(2,1)}, bf16[1,2,16384]{2,1,0:T(2,128)(2,1)S(1)}, u32[]{:S(2)}, u32[]{:S(2)}) collective-permute-start(bf16[1,2,16384]{2,1,0:T(2,128)(2,1)} %param.6), channel_id=1, source_target_pairs={{0,2},{2,0},{4,6},{6,4},{8,10},{10,8},{12,14},{14,12},{1,3},{3,1},... | collective-permute-start | bytes 196616 | tf_op jit(solution)/shard_map/ppermute | solution.py:139
  5.8 1.3 %copy.65 = bf16[8,2,16384]{2,1,0:T(2,128)(2,1)} copy(bf16[8,2,16384]{2,0,1:T(8,128)(2,1)S(1)} %pad_maximum_fusion) | data formatting | bytes 1048576 | tf_op jit(solution)/shard_map/stack | solution.py:131
  7.1 4.9 %all-to-all-start = ((bf16[8,2,16384]{2,1,0:T(2,128)(2,1)}), bf16[8,2,16384]{2,1,0:T(2,128)(2,1)S(1)}, u32[]{:S(2)}, u32[]{:S(2)}) async-start(bf16[8,2,16384]{2,1,0:T(2,128)(2,1)} %copy.65), calls=%async_computation | async-start | bytes 1048576 | tf_op jit(solution)/shard_map/all_to_all | solution.py:132
  16.0 2.1 %collective-permute-start.1 = (bf16[1,2,32768]{2,1,0:T(2,128)(2,1)S(1)}, bf16[1,2,32768]{2,1,0:T(2,128)(2,1)S(1)}, u32[]{:S(2)}, u32[]{:S(2)}) collective-permute-start(bf16[1,2,32768]{2,1,0:T(2,128)(2,1)S(1)} %broadcast_select_fusion.3), channel_id=1, source_target_pairs={{0,4},{2,6},{4,0},{6,2},{8,12},{10,14},{12,8},{14,10},{1,5},{3,7},... | collective-permute-start | bytes 393224 | tf_op jit(solution)/shard_map/ppermute | solution.py:139
  18.3 6.5 %collective-permute-done.1 = bf16[1,2,32768]{2,1,0:T(2,128)(2,1)S(1)} collective-permute-done((bf16[1,2,32768]{2,1,0:T(2,128)(2,1)S(1)}, bf16[1,2,32768]{2,1,0:T(2,128)(2,1)S(1)}, u32[]{:S(2)}, u32[]{:S(2)}) %collective-permute-start.1) | collective-permute-done | bytes 131104 | tf_op jit(solution)/shard_map/ppermute | solution.py:139
  25.2 3.0 %collective-permute-start.2 = (bf16[1,2,65536]{2,1,0:T(2,128)(2,1)S(1)}, bf16[1,2,65536]{2,1,0:T(2,128)(2,1)S(1)}, u32[]{:S(2)}, u32[]{:S(2)}) collective-permute-start(bf16[1,2,65536]{2,1,0:T(2,128)(2,1)S(1)} %broadcast_select_fusion.1), channel_id=1, source_target_pairs={{0,8},{2,10},{4,12},{6,14},{8,0},{10,2},{12,4},{14,6},{1,9},{3,11}... | collective-permute-start | bytes 786440 | tf_op jit(solution)/shard_map/ppermute | solution.py:139
  28.6 10.4 %collective-permute-done.2 = bf16[1,2,65536]{2,1,0:T(2,128)(2,1)S(1)} collective-permute-done((bf16[1,2,65536]{2,1,0:T(2,128)(2,1)S(1)}, bf16[1,2,65536]{2,1,0:T(2,128)(2,1)S(1)}, u32[]{:S(2)}, u32[]{:S(2)}) %collective-permute-start.2) | collective-permute-done | bytes 262176 | tf_op jit(solution)/shard_map/ppermute | solution.py:139
  39.8 4.1 %fusion.81 = (f32[131072]{0:T(1024)S(1)}, f32[131072]{0:T(1024)S(1)}, f32[]{:T(128)}, f32[1,1,131072]{2,1,0:T(1,128)S(1)}) fusion(bf16[1,2,131072]{2,1,0:T(2,128)(2,1)S(1)} %broadcast_select_fusion), kind=kLoop, calls=%fused_computation.189 | loop fusion | flops 786431 | bytes 2097156 | tf_op jit(solution)/shard_map/convert_element_type | solution.py:75
  45.4 2.9 %select_reduce_fusion.3 = (f32[]{:T(128)}, f32[]{:T(128)}, f32[]{:T(128)}, f32[]{:T(128)}) fusion(f32[131072]{0:T(1024)S(1)} %bitcast.316, s32[]{:T(128)} %bitcast.4, s32[]{:T(128)} %bitcast.3, s32[]{:T(128)} %bitcast.2), kind=kLoop, calls=%fused_computation.156 | loop fusion | flops 2621436 | bytes 524316 | tf_op jit(solution)/shard_map/reduce_sum | solution.py:91
  57.3 4.6 %fusion.79 = (bf16[8,8,32,128]{3,1,2,0:T(8,128)(2,1)S(1)}, bf16[8,8,32,128]{3,1,2,0:T(8,128)(2,1)S(1)}) fusion(f32[2,64,4096]{2,1,0:T(8,128)S(1)} %fusion.57), kind=kLoop, calls=%fused_computation.185 | loop fusion | flops 5767168 | bytes 3145728
  63.6 1.1 copy.71
  65.1 1.1 copy.70
  66.5 3.2 %select_convert_fusion.5 = (bf16[1,32,4096]{2,1,0:T(8,128)(2,1)S(1)}, bf16[1,32,4096]{2,1,0:T(8,128)(2,1)S(1)}, bf16[1,32,4096]{2,1,0:T(8,128)(2,1)S(1)}, bf16[1,32,4096]{2,1,0:T(8,128)(2,1)S(1)}) fusion(s32[]{:T(128)} %bitcast.4, s32[]{:T(128)} %bitcast.3, s32[]{:T(128)} %bitcast.2, f32[1,32,4096]{2,1,0:T(8,128)S(1)} %squeeze.55, ...), kind=kLoop, calls=%fused_computation.171 | loop fusion | flops 2752512 | bytes 3145740 | tf_op jit(solution)/shard_map/convert.25
  69.7 2.3 %select_convert_fusion.6 = (bf16[1,32,4096]{2,1,0:T(8,128)(2,1)S(1)}, bf16[1,32,4096]{2,1,0:T(8,128)(2,1)S(1)}, bf16[1,32,4096]{2,1,0:T(8,128)(2,1)S(1)}, bf16[1...) fusion(bf16[1,32,4096]{2,1,0:T(8,128)(2,1)S(1)} %get-tuple-element.42, ...), kind=kLoop, calls=%fused_computation.172 | loop fusion | flops 2490368 | bytes 2097164 | tf_op jit(solution)/shard_map/convert.50
  72.5 4.6 %fusion.49 = (bf16[8,8,32,128]{3,1,2,0:T(8,128)(2,1)S(1)}, bf16[8,8,32,128]{3,1,2,0:T(8,128)(2,1)S(1)}) fusion(f32[2,64,4096]{2,1,0:T(8,128)S(1)} %convolution_bitcast_fusion.3), kind=kLoop, calls=%fused_computation.115 | loop fusion | flops 5767168 | bytes 3145728
  77.8 4.6 %fusion.51 = (bf16[8,8,32,128]{3,1,2,0:T(8,128)(2,1)S(1)}, bf16[8,8,32,128]{3,1,2,0:T(8,128)(2,1)S(1)}) fusion(f32[2,64,4096]{2,1,0:T(8,128)S(1)} %convolution_bitcast_fusion.2), kind=kLoop, calls=%fused_computation.117 | loop fusion | flops 5767168 | bytes 3145728
  83.2 4.6 %fusion.53 = (bf16[8,8,32,128]{3,1,2,0:T(8,128)(2,1)S(1)}, bf16[8,8,32,128]{3,1,2,0:T(8,128)(2,1)S(1)}) fusion(f32[2,64,4096]{2,1,0:T(8,128)S(1)} %convolution_bitcast_fusion.1), kind=kLoop, calls=%fused_computation.119 | loop fusion | flops 5767168 | bytes 3145728
  88.5 4.8 %fusion.55 = (bf16[8,8,32,128]{3,1,2,0:T(8,128)(2,1)S(1)}, bf16[8,8,32,128]{3,1,2,0:T(8,128)(2,1)S(1)}) fusion(f32[2,64,4096]{2,1,0:T(8,128)S(1)} %convolution_bitcast_fusion), kind=kLoop, calls=%fused_computation.121 | loop fusion | flops 5767168 | bytes 3145728
  95.5 1.3 %subtract_convert_fusion.4 = (bf16[1,64,32,128]{3,2,0,1:T(8,128)(2,1)S(1)}, bf16[1,64,32,128]{3,2,0,1:T(8,128)(2,1)S(1)}, bf16[1,64,32,128]{3,2,0,1:T(8,128)(2,1...) fusion(f32[2,64,32,128]{3,2,0,1:T(8,128)S(1)} %convolution_bitc, ...), kind=kLoop, calls=%fused_computation.90 | loop fusion | flops 8388608 | bytes 12615680 | tf_op jit(solution)/shard_map/convert.19
  98.7 2.4 %broadcast_multiply_fusion = (f32[1,64,32,64]{1,2,0,3:T(8,128)S(1)}, bf16[1,64,32,64]{1,2,0,3:T(8,128)(2,1)}, bf16[1,64,32,64]{1,2,0,3:T(8,128)(2,1)}, f32[1,64,32,64]{1,2,0,3:T(8,128)S(1)}) fusion(f32[]{:T(128)S(6)} %div.55, f32[2,64,32,64]{1,2,0,3:T(8,128)S(1)} %get-tuple-element.79, f32[]{:T(128)S(6)} %div.59, f32[2,64,32,64]{1,2,0,3:T(8,128)S(1)} %fusion.1, ...), kind=kLoop, calls=%fused_computation.152 | loop fusion | flops 5111808 | bytes 6815764 | tf_op jit(solution)/shard_map/div | solution.py:103
  101.2 1.1 copy.86
  103.3 2.1 %copy.85 = bf16[1,64,32,64]{3,2,1,0:T(8,128)(2,1)S(1)} copy(bf16[1,64,32,64]{1,2,0,3:T(8,128)(2,1)} %get-tuple-element.12) | data formatting | bytes 524288 | tf_op jit(solution)/shard_map/convert_element_type | solution.py:106
  106.5 1.1 copy.84
  108.6 1.1 copy.87
  (100 shorter events, 25.8 us)
Async XLA Ops:
  0.6 15.2 %collective-permute-start = (bf16[1,2,16384]{2,1,0:T(2,128)(2,1)}, bf16[1,2,16384]{2,1,0:T(2,128)(2,1)S(1)}, u32[]{:S(2)}, u32[]{:S(2)}) collective-permute-start(bf16[1,2,16384]{2,1,0:T(2,128)(2,1)} %param.6), channel_id=1, source_target_pairs={{0,2},{2,0},{4,6},{6,4},{8,10},{10,8},{12,14},{14,12},{1,3},{3,1},... | collective-permute-start | bytes 196616 | tf_op jit(solution)/shard_map/ppermute | solution.py:139
  4.7 10.1 %copy-start.4 = (s32[8,8]{1,0:T(8,128)S(1)}, s32[8,8]{1,0:T(8,128)}, u32[]{:S(2)}) copy-start(s32[8,8]{1,0:T(8,128)} %param.5) | copy-start | bytes 772
  4.7 10.5 %copy-start.5 = (s32[1,3]{1,0:T(1,128)S(1)}, s32[1,3]{1,0:T(1,128)}, u32[]{:S(2)}) copy-start(s32[1,3]{1,0:T(1,128)} %param.7) | copy-start | bytes 40
  4.7 11.1 %copy-start.3 = (bf16[1,2,16384]{2,1,0:T(2,128)(2,1)S(1)}, bf16[1,2,16384]{2,1,0:T(2,128)(2,1)}, u32[]{:S(2)}) copy-start(bf16[1,2,16384]{2,1,0:T(2,128)(2,1)} %param.6) | copy-start | bytes 196612
  7.1 47.5 %all-to-all-start = ((bf16[8,2,16384]{2,1,0:T(2,128)(2,1)}), bf16[8,2,16384]{2,1,0:T(2,128)(2,1)S(1)}, u32[]{:S(2)}, u32[]{:S(2)}) async-start(bf16[8,2,16384]{2,1,0:T(2,128)(2,1)} %copy.65), calls=%async_computation | async-start | bytes 1048576 | tf_op jit(solution)/shard_map/all_to_all | solution.py:132
  16.0 8.8 %collective-permute-start.1 = (bf16[1,2,32768]{2,1,0:T(2,128)(2,1)S(1)}, bf16[1,2,32768]{2,1,0:T(2,128)(2,1)S(1)}, u32[]{:S(2)}, u32[]{:S(2)}) collective-permute-start(bf16[1,2,32768]{2,1,0:T(2,128)(2,1)S(1)} %broadcast_select_fusion.3), channel_id=1, source_target_pairs={{0,4},{2,6},{4,0},{6,2},{8,12},{10,14},{12,8},{14,10},{1,5},{3,7},... | collective-permute-start | bytes 393224 | tf_op jit(solution)/shard_map/ppermute | solution.py:139
  25.2 13.8 %collective-permute-start.2 = (bf16[1,2,65536]{2,1,0:T(2,128)(2,1)S(1)}, bf16[1,2,65536]{2,1,0:T(2,128)(2,1)S(1)}, u32[]{:S(2)}, u32[]{:S(2)}) collective-permute-start(bf16[1,2,65536]{2,1,0:T(2,128)(2,1)S(1)} %broadcast_select_fusion.1), channel_id=1, source_target_pairs={{0,8},{2,10},{4,12},{6,14},{8,0},{10,2},{12,4},{14,6},{1,9},{3,11}... | collective-permute-start | bytes 786440 | tf_op jit(solution)/shard_map/ppermute | solution.py:139
  65.1 1.5 %copy-start = (f32[1,32,4096]{2,1,0:T(8,128)S(1)}, f32[1,32,4096]{2,1,0:T(8,128)}, u32[]{:S(2)}) copy-start(f32[1,32,4096]{2,1,0:T(8,128)} %reshape.1495) | copy-start | bytes 1572868
  102.2 4.2 %copy-start.1 = (bf16[1,64,32,64]{1,2,0,3:T(8,128)(2,1)S(1)}, bf16[1,64,32,64]{1,2,0,3:T(8,128)(2,1)}, u32[]{:S(2)}) copy-start(bf16[1,64,32,64]{1,2,0,3:T(8,128)(2,1)} %get-tuple-element.31) | copy-start | bytes 786436
  108.6 1.3 %copy-start.2 = (f32[131072]{0:T(1024)S(1)}, f32[131072]{0:T(1024)}, u32[]{:S(2)}) copy-start(f32[131072]{0:T(1024)} %reshape.1590) | copy-start | bytes 1572868
